TPU v7x, 32 devices: a whole 2x2x4 slice. The times are simulated.
32 devices in a mesh: row: 4 (over z), col: 8 (over y, x, core).
Axes of the slice: x: 2, y: 2, z: 4, core: 2. Of those that a mesh axis runs over, the one named last changes fastest.
Arguments:
- queries: bfloat16 [4, 1024, 512], P('row', 'col'), may hold values from -6 to 6
- keys: bfloat16 [8, 512, 512], P('col', 'row'), may hold values from -6 to 6
- values: bfloat16 [8, 512, 512], P('col', 'row'), may hold values from -6 to 6
- outputs: bfloat16 [4, 1024, 512], P('row', 'col'), may hold values from -2 to 2
- grad_out: bfloat16 [4, 1024, 512], P('row', 'col'), may hold values from -48 to 48
- lse: float32 [4, 8, 1024], P('row'), may hold values from 7 to 9.5
- tile_slot: int32 [4, 8, 24], P('row', 'col'), may hold values from 0 to 31, as said below
- tile_live: int32 [4, 8], P('row', 'col'), may hold values from 1 to 24, as said below
- tile_bits: int32 [4, 8, 24, 8, 128], P('row', 'col'), may hold values from 0 to 65535, as said below
Outputs:
- grad_queries: bfloat16 [4, 1024, 512], P('row', 'col')
- grad_keys: bfloat16 [8, 512, 512], P('col', 'row')
- grad_values: bfloat16 [8, 512, 512], P('col', 'row')
Inputs may be any that keep to these rules, and one draw needn't show every extreme that they name: `tile_slot`: the 24 entries of one pair of blocks are distinct slots. `tile_live`: some pair of blocks has all 24 entries live. `tile_bits`: each word holds 16 edge bits in its low bits.
All inputs are finite; a program needn't handle non-finite values.
Results may differ from a plain program's by a relative error of at most 0.02.
Values may be sent and summed in bfloat16 or wider, within the bound.
No kernel may reach another device: no remote copies, remote signals or barrier semaphores. Data moves between devices by JAX's collectives and lax.ppermute only.
A program may use at most 64 MiB of HBM per device.

v0:
```python
import functools

import jax
import jax.numpy as jnp
from jax import lax
from jax.experimental import pallas as pl
from jax.experimental.pallas import tpu as pltpu
from jax.sharding import Mesh
from jax.sharding import PartitionSpec as P


F32 = jnp.float32
BF16 = jnp.bfloat16
I32 = jnp.int32
LANES = 128
PAD = 16
QUARTERS = 4
TOGETHER = 8
LSE_UNIT = 2.0**21
NT = (((1,), (1,)), ((), ()))
NN = (((1,), (0,)), ((), ()))
MEDIUM = pltpu.CompilerParams(vmem_limit_bytes=28 * 1024 * 1024)
PACK = pltpu.CompilerParams(vmem_limit_bytes=int(53.6 * 1024 * 1024))
SMALL = pltpu.CompilerParams(vmem_limit_bytes=12 * 1024 * 1024)
def early(gigaflops):
    return pl.CostEstimate(flops=gigaflops * 10**9, bytes_accessed=0, transcendentals=0)


VMEM = pl.BlockSpec(memory_space=pltpu.VMEM)
HBM = pl.BlockSpec(memory_space=pltpu.HBM)


def lanes_of(quarter):
    return pl.ds(pl.multiple_of(quarter * LANES, LANES), LANES)


def my_place():
    row, chip, core = (lax.axis_index(name) for name in ("row", "chip", "core"))
    return row, chip, core, row % 2 * 2 + core


def pack_kernel(
    heads, q_hbm, g_hbm, o_hbm, k_hbm, v_hbm, bits_hbm, lse_hbm, slot_ref, live_ref,
    qg_own, pair0_ref, pair1_ref, kv_own, sib_ref, packed_ref, lse_own,
    q_ref, g_ref, o_ref, k_ref, v_ref, bits_ref, lse_ref, delta_ref, sems,
):
    arrays = (
        (q_hbm, q_ref), (g_hbm, g_ref), (o_hbm, o_ref), (k_hbm, k_ref),
        (v_hbm, v_ref), (bits_hbm, bits_ref), (lse_hbm, lse_ref),
    )
    copies = [pltpu.make_async_copy(a, b, sems.at[i]) for i, (a, b) in enumerate(arrays)]
    for copy in copies:
        copy.start()
    rows, width = q_ref.shape[1:]
    krows = k_ref.shape[1]
    head_dim = width // heads
    local = heads // QUARTERS
    capacity = bits_ref.shape[2]
    quarter = my_place()[3]
    feature = lax.broadcasted_iota(I32, (QUARTERS * PAD, width), 1)
    line = lax.broadcasted_iota(I32, (QUARTERS * PAD, width), 0)
    wanted = jnp.where(line % PAD < local, line // PAD * local + line % PAD, -1)
    pick = (feature // head_dim == wanted).astype(F32)
    packed_ref[capacity // 2] = jnp.zeros((8, LANES), I32)
    packed_ref[capacity // 2, 0:1, 0:capacity] = slot_ref[0]
    packed_ref[capacity // 2, 1:2, 0:1] = live_ref[...]
    for copy in copies:
        copy.wait()
    product = g_ref[0].astype(F32) * o_ref[0].astype(F32)
    delta = lax.dot_general(
        pick, product, NT, precision=lax.Precision.HIGHEST, preferred_element_type=F32
    ).astype(BF16)
    for index in range(QUARTERS):
        delta_ref[index] = delta[index * PAD : (index + 1) * PAD]
    for step, (ref, start) in enumerate(
        ((qg_own, 0), (sib_ref, 4 * krows), (pair0_ref, 0), (pair1_ref, 0))
    ):
        lanes = lanes_of(quarter ^ step)
        ref[start : start + rows] = q_ref[0, :, lanes]
        ref[start + rows : start + 2 * rows] = g_ref[0, :, lanes]
        if rows < LANES:
            ref[start + 2 * rows : start + 2 * rows + PAD] = jnp.zeros((PAD, LANES), BF16)
        ref[start + 2 * rows : start + 2 * rows + PAD, :rows] = delta_ref[quarter ^ step]
    for step in range(QUARTERS):
        ref = (kv_own, sib_ref)[step % 2]
        lanes = lanes_of(quarter ^ step)
        start = step // 2 * 2 * krows
        ref[start : start + krows] = k_ref[0, :, lanes]
        ref[start + krows : start + 2 * krows] = v_ref[0, :, lanes]
    every = lse_ref[0]

    def lse_of(wanted_quarter):
        own = every[:local]
        for index in range(1, QUARTERS):
            own = jnp.where(
                wanted_quarter == index, every[local * index : local * (index + 1)], own
            )
        return own

    mine = lse_of(quarter)
    other = (lse_of(quarter ^ 2) * LSE_UNIT).astype(I32)
    for u in range(lse_own.shape[0]):
        lanes = slice(u * LANES, (u + 1) * LANES)
        lse_own[u] = mine[:, lanes]
        packed_ref[capacity // 2 + 1 + u // 4, u % 4 * 2 : u % 4 * 2 + 2] = other[:, lanes]
    for entry in range(capacity):
        words = bits_ref[0, 0, entry]
        span = slice(entry % 2 * 4, entry % 2 * 4 + 4)
        packed_ref[entry // 2, span] = words[:4] | lax.shift_left(words[4:], I32(16))


def key_join_kernel(krows, kv_own, sib_ref, kv_same, kv_pair):
    core = my_place()[2]
    for side, ref in enumerate((kv_same, kv_pair)):
        span = slice(side * 2 * krows, (side + 1) * 2 * krows)
        ref[core] = kv_own[span]
        ref[1 - core] = sib_ref[span]


def query_join_kernel(
    krows, slabs, qg_own, sib_ref, pair0_ref, pair1_ref, bits_own, bits_pair, lse_own,
    qg_out, bits_out, lse_out,
):
    row, chip, core, quarter = my_place()
    side = row % 2
    qg_out[quarter] = qg_own[...]
    qg_out[quarter ^ 1] = sib_ref[4 * krows :]
    qg_out[quarter ^ 2] = pair0_ref[...]
    qg_out[quarter ^ 3] = pair1_ref[...]
    bits_out[side] = bits_own[:slabs]
    bits_out[1 - side] = bits_pair[:slabs]
    lse_out[side] = lse_own[...]
    for u in range(lse_out.shape[1]):
        fixed = bits_pair[slabs + u // 4, u % 4 * 2 : u % 4 * 2 + 2]
        lse_out[1 - side, u] = fixed.astype(F32) * (1.0 / LSE_UNIT)


def far_join_kernel(pair_ref, *refs):
    parts, (far_out, pair_out) = refs[:-2], refs[-2:]
    for index, ref in enumerate(parts):
        far_out[index] = ref[...]
    pair_out[...] = pair_ref[...]


def key_place_kernel(head_dim, tile, same_ref, pair_ref, far_ref, k_out, v_out, k2t_out):
    kv_refs = [same_ref, pair_ref] + [far_ref.at[index] for index in range(far_ref.shape[0])]
    krows = kv_refs[0].shape[1] // 2
    row = my_place()[0]
    for step, ref in enumerate(kv_refs):
        start = (row ^ step) * krows
        inner = pl.multiple_of(start % tile, krows)
        for block in range(2):
            k_out[block, start // tile, pl.ds(inner, krows)] = ref[block, :krows]
            v_out[block, start // tile, pl.ds(inner, krows)] = ref[block, krows:]
    low_row = lax.broadcasted_iota(I32, (LANES, tile), 0) < head_dim
    none_t = jnp.zeros((LANES, tile), BF16)
    for block in range(2):
        for w in range(k_out.shape[1]):
            flipped = k_out[block, w].T
            k2t_out[block, w] = jnp.concatenate(
                [jnp.where(low_row, flipped, none_t), jnp.where(low_row, none_t, flipped)], axis=1
            )


def pair_kernel(sizes, *refs):
    head_dim, tile, capacity, chips, row_count = sizes
    qg_refs, refs = refs[:chips], refs[chips:]
    (k_scr, v_scr, k2t_scr), refs = refs[:3], refs[3:]
    bits_refs, lse_ref, refs = refs[:2], refs[2], refs[3:]
    dqt_ref, dkv_refs, refs = refs[0], refs[1 : 1 + row_count], refs[1 + row_count :]
    q2_scr, g2_scr, delta_scr, dqt_scr, dk_scr, dv_scr, bits_scr, info, todo, sems = refs
    rows = (qg_refs[0].shape[1] - PAD) // 2
    krows = dkv_refs[0].shape[1] // 2
    query_tiles = q2_scr.shape[1]
    key_tiles = k_scr.shape[1]
    scaling = float(head_dim) ** -0.5
    row, chip, core, quarter = my_place()
    side = row % 2

    copies = [
        pltpu.make_async_copy(
            bits_refs[i % 2].at[i // 2, capacity // 2], info.at[i], sems.at[i]
        )
        for i in range(QUARTERS)
    ]
    for copy in copies:
        copy.start()

    low = lax.broadcasted_iota(I32, (rows, LANES), 1) < head_dim
    none = jnp.zeros((rows, LANES), BF16)
    for step in range(chips):
        for index in range(QUARTERS):
            source = (chip ^ step) * 2 + index % 2
            start = source * rows
            u = start // tile
            inner = pl.multiple_of(start % tile, rows)
            block = index // 2
            for scr, part in ((q2_scr, 0), (g2_scr, 1)):
                piece = qg_refs[step][index, part * rows : (part + 1) * rows]
                if part == 0:
                    piece = (piece.astype(F32) * scaling).astype(BF16)
                scr[block, u, 0, pl.ds(inner, rows)] = jnp.where(low, piece, none)
                scr[block, u, 1, pl.ds(inner, rows)] = jnp.where(low, none, piece)
            delta = qg_refs[step][index, 2 * rows :, :rows].astype(F32)
            if rows == tile:
                delta_scr[block, u] = delta
            else:
                for part in range(tile // rows):
                    @pl.when(source % (tile // rows) == part)
                    def _(part=part, delta=delta, u=u, block=block):
                        delta_scr[block, u, :, part * rows : (part + 1) * rows] = delta
    dqt_scr[...] = jnp.zeros_like(dqt_scr)
    dk_scr[...] = jnp.zeros_like(dk_scr)
    dv_scr[...] = jnp.zeros_like(dv_scr)
    place_in = lax.broadcasted_iota(I32, (2, 4, 16, tile), 2)
    upper = lax.broadcasted_iota(I32, (2, 4, 16, tile), 0)
    bit = lax.shift_left(I32(1), place_in + 16 * upper).reshape(tile, tile)
    for step in range(QUARTERS):
        for entry in range(capacity):
            span = slice(entry % 2 * 4, entry % 2 * 4 + 4)
            bits_scr[step, entry] = bits_refs[step % 2][side ^ (step // 2), entry // 2, span]
    for i, copy in enumerate(copies):
        copy.wait()
    count = I32(0)
    for i in range(QUARTERS):
        step = (side ^ (i // 2)) * 2 + i % 2

        def listed(entry, count, i=i, step=step):
            todo[count] = info[i, 0, entry] + 32 * entry + 1024 * step
            return count + 1

        count = lax.fori_loop(0, info[i, 1, 0], listed, count)

    def some_tiles(index, _):
        work = []
        for part in range(TOGETHER):
            position = index * TOGETHER + part
            item = todo[jnp.minimum(position, count - 1)]
            slot = item % 32
            step = item // 1024
            qb = side ^ (step // 2)
            kb = core ^ (step % 2)
            u = slot // key_tiles
            w = slot % key_tiles
            words = bits_scr[step, item // 32 % 32]
            if part:
                words = words & jnp.where(position < count, I32(-1), I32(0))
            words = jnp.broadcast_to(words[:, None, :], (4, 16, tile)).reshape(64, tile)
            edge = (jnp.concatenate([words, words], axis=0) & bit) != 0
            q2 = q2_scr[qb, u].reshape(2 * tile, LANES)
            g2 = g2_scr[qb, u].reshape(2 * tile, LANES)
            scores = lax.dot_general(k_scr[kb, w], q2, NT, preferred_element_type=F32)
            grad_prob = lax.dot_general(v_scr[kb, w], g2, NT, preferred_element_type=F32)
            work.append((qb, kb, u, w, edge, q2, g2, scores, grad_prob))
        done = []
        for qb, kb, u, w, edge, q2, g2, scores, grad_prob in work:
            lse_tile = lse_ref[qb, u]
            delta_tile = delta_scr[qb, u]
            probs, grads = [], []
            for h in range(2):
                s = scores[:, h * tile : (h + 1) * tile]
                gp = grad_prob[:, h * tile : (h + 1) * tile]
                p = jnp.where(edge, jnp.exp(s - lse_tile[h : h + 1]), 0.0)
                ds = p * (gp - delta_tile[h : h + 1])
                probs.append(p.astype(BF16))
                grads.append(ds.astype(BF16))
            done.append((
                lax.dot_general(
                    jnp.concatenate(probs, axis=1), g2, NN, preferred_element_type=F32
                ),
                lax.dot_general(
                    jnp.concatenate(grads, axis=1), q2, NN, preferred_element_type=F32
                ),
                lax.dot_general(
                    k2t_scr[kb, w], jnp.concatenate(grads, axis=0), NN,
                    preferred_element_type=F32,
                ),
            ))
        for (qb, kb, u, w, *_), (dv, dk, dqt) in zip(work, done):
            dv_scr[kb, w] += dv
            dk_scr[kb, w] += dk
            dqt_scr[qb, u] += dqt
        return 0

    lax.fori_loop(0, (count + TOGETHER - 1) // TOGETHER, some_tiles, 0)

    for step in range(row_count):
        start = (row ^ step) * krows
        inner = pl.multiple_of(start % tile, krows)
        for block in range(2):
            dk = dk_scr[block, start // tile, pl.ds(inner, krows)]
            dv = dv_scr[block, start // tile, pl.ds(inner, krows)]
            dkv_refs[step][block, :krows] = dk.astype(BF16)
            dkv_refs[step][block, krows:] = dv.astype(BF16)
    dqt_ref[...] = (dqt_scr[...] * scaling).astype(BF16)


def turn_kernel(rows, dqt_ref, *refs):
    dq_refs, dq_scr = refs[:-1], refs[-1]
    tile = dqt_ref.shape[3]
    chip = my_place()[1]
    for block in range(2):
        for u in range(dqt_ref.shape[1]):
            dq_scr[block, u * tile : (u + 1) * tile] = dqt_ref[block, u].T
    for step, ref in enumerate(dq_refs):
        for index in range(QUARTERS):
            start = pl.multiple_of(((chip ^ step) * 2 + index % 2) * rows, rows)
            ref[index] = dq_scr[index // 2, pl.ds(start, rows)]


def query_sum_kernel(chips, *refs):
    parts, (same_ref, pair_ref) = refs[:chips], refs[chips:]
    side = my_place()[0] % 2
    for step, ref in enumerate((same_ref, pair_ref)):
        for core in range(2):
            index = (side ^ step) * 2 + core
            total = parts[0][index].astype(F32)
            for part in parts[1:]:
                total += part[index].astype(F32)
            ref[core] = total.astype(BF16)


def key_sum_kernel(row_count, *refs):
    dkv_refs, (own_ref, sib_ref) = refs[:1] + refs[row_count - 1 : 0 : -1], refs[-2:]
    core = my_place()[2]
    for ref, block in ((own_ref, core), (sib_ref, 1 - core)):
        for side in range(2):
            total = dkv_refs[side][block].astype(F32)
            for other in range(side + 2, row_count, 2):
                total += dkv_refs[other][block].astype(F32)
            ref[side] = total.astype(BF16)


def bundle_kernel(dkv_ref, dq_same, dq_pair, out):
    krows2 = dkv_ref.shape[1]
    sibling = 1 - my_place()[2]
    out[:, :krows2] = dkv_ref[...]
    for side, dq in enumerate((dq_same, dq_pair)):
        out[side, krows2:] = dq[sibling]


def finish_kernel(krows, dkv_own, dq_same, dq_pair, sib_ref, dq_out, dk_out, dv_out):
    row, chip, core, quarter = my_place()
    for side, dq in enumerate((dq_same, dq_pair)):
        for step, ref in enumerate((dkv_own, sib_ref)):
            lanes = lanes_of(quarter ^ (2 * side + step))
            dk_out[0, :, lanes] = ref[side, :krows]
            dv_out[0, :, lanes] = ref[side, krows : 2 * krows]
            dq_out[0, :, lanes] = ref[side, 2 * krows :] if step else dq[core]


def send(block, axes, count, step):
    return lax.ppermute(block, axes, [(place, place ^ step) for place in range(count)])


def body(sizes, queries, keys, values, outputs, grad_out, lse, tile_slot, tile_live, tile_bits):
    row_count, chips, cores = sizes
    heads = lse.shape[1]
    width = queries.shape[2]
    head_dim = width // heads
    tile = tile_bits.shape[4]
    capacity = tile_slot.shape[2]
    rows = queries.shape[1]
    krows = keys.shape[1]
    query_tiles = lse.shape[2] // tile
    key_tiles = row_count * krows // tile
    line = ("row", "core")
    places = row_count * cores

    def shape(*dims, dtype=BF16):
        return jax.ShapeDtypeStruct(dims, dtype)

    qg_shape = shape(2 * rows + PAD, LANES)
    kv_shape = shape(2, 2 * krows, LANES)
    slabs = capacity // 2 + 1
    qg_own, pair0, pair1, kv_own, to_sibling, bits_own, lse_own = pl.pallas_call(
        functools.partial(pack_kernel, heads),
        out_shape=(
            qg_shape, qg_shape, qg_shape, shape(4 * krows, LANES),
            shape(4 * krows + 2 * rows + PAD, LANES),
            shape(slabs + query_tiles // 4, 8, LANES, dtype=I32),
            shape(query_tiles, 2, tile, dtype=F32),
        ),
        in_specs=[HBM] * 7 + [VMEM] * 2,
        out_specs=(VMEM,) * 7,
        scratch_shapes=[
            pltpu.VMEM(queries.shape, BF16),
            pltpu.VMEM(queries.shape, BF16),
            pltpu.VMEM(queries.shape, BF16),
            pltpu.VMEM(keys.shape, BF16),
            pltpu.VMEM(keys.shape, BF16),
            pltpu.VMEM(tile_bits.shape, I32),
            pltpu.VMEM(lse.shape, F32),
            pltpu.VMEM((QUARTERS, PAD, rows), BF16),
            pltpu.SemaphoreType.DMA((7,)),
        ],
        compiler_params=PACK,
        name="pack",
    )(queries, grad_out, outputs, keys, values, tile_bits, lse, tile_slot, tile_live)

    pair0 = send(pair0, line, places, 2)
    pair1 = send(pair1, line, places, 3)
    from_sibling = send(to_sibling, "core", cores, 1)
    bits_pair = send(bits_own, "row", row_count, 1)
    kv_same, kv_pair = pl.pallas_call(
        functools.partial(key_join_kernel, krows),
        out_shape=(kv_shape, kv_shape),
        in_specs=[VMEM] * 2,
        out_specs=(VMEM,) * 2,
        compiler_params=SMALL,
        name="key_join",
    )(kv_own, from_sibling)
    kv_out = (kv_same, kv_pair)
    kv_far, kv_pair = pl.pallas_call(
        far_join_kernel,
        out_shape=(shape(row_count - 2, *kv_shape.shape), kv_shape),
        in_specs=[VMEM] * (row_count - 1),
        out_specs=(VMEM, VMEM),
        compiler_params=SMALL,
        cost_estimate=early(20),
        name="far_join",
    )(kv_pair, *[send(kv_out[step % 2], "row", row_count, step) for step in range(2, row_count)])
    kv = (kv_same, send(kv_pair, "row", row_count, 1), kv_far)
    qg, bits, lse2 = pl.pallas_call(
        functools.partial(query_join_kernel, krows, slabs),
        out_shape=(
            shape(QUARTERS, 2 * rows + PAD, LANES),
            shape(2, capacity // 2 + 1, 8, LANES, dtype=I32),
            shape(2, query_tiles, 2, tile, dtype=F32),
        ),
        in_specs=[VMEM] * 7,
        out_specs=(VMEM,) * 3,
        compiler_params=SMALL,
        cost_estimate=early(20),
        name="query_join",
    )(qg_own, from_sibling, pair0, pair1, bits_own, bits_pair, lse_own)
    qg = [qg] + [send(qg, "chip", chips, step) for step in range(1, chips)]
    bits_sibling = send(bits, "core", cores, 1)

    placed = pl.pallas_call(
        functools.partial(key_place_kernel, head_dim, tile),
        out_shape=(
            shape(2, key_tiles, tile, LANES), shape(2, key_tiles, tile, LANES),
            shape(2, key_tiles, LANES, 2 * tile),
        ),
        in_specs=[VMEM] * 3,
        out_specs=(VMEM,) * 3,
        compiler_params=SMALL,
        name="key_place",
    )(*kv)
    parts = pl.pallas_call(
        functools.partial(pair_kernel, (head_dim, tile, capacity, chips, row_count)),
        out_shape=(shape(2, query_tiles, LANES, tile),) + (kv_shape,) * row_count,
        in_specs=[VMEM] * (chips + 6),
        out_specs=(VMEM,) * (1 + row_count),
        scratch_shapes=[
            pltpu.VMEM((2, query_tiles, 2, tile, LANES), BF16),
            pltpu.VMEM((2, query_tiles, 2, tile, LANES), BF16),
            pltpu.VMEM((2, query_tiles, PAD, tile), F32),
            pltpu.VMEM((2, query_tiles, LANES, tile), F32),
            pltpu.VMEM((2, key_tiles, tile, LANES), F32),
            pltpu.VMEM((2, key_tiles, tile, LANES), F32),
            pltpu.VMEM((QUARTERS, capacity, 4, LANES), I32),
            pltpu.SMEM((QUARTERS, 8, LANES), I32),
            pltpu.SMEM((QUARTERS * capacity,), I32),
            pltpu.SemaphoreType.DMA((QUARTERS,)),
        ],
        compiler_params=MEDIUM,
        name="pair",
    )(*qg, *placed, bits, bits_sibling, lse2)

    dkv = parts[1:]
    dq = pl.pallas_call(
        functools.partial(turn_kernel, rows),
        out_shape=(shape(QUARTERS, rows, LANES),) * chips,
        in_specs=[VMEM],
        out_specs=(VMEM,) * chips,
        scratch_shapes=[pltpu.VMEM((2, query_tiles * tile, LANES), BF16)],
        compiler_params=SMALL,
        name="turn",
    )(parts[0])
    dq = [dq[0]] + [send(dq[step], "chip", chips, step) for step in range(1, chips)]
    dkv = [dkv[0]] + [
        send(dkv[step], "row", row_count, step) for step in range(row_count - 1, 0, -1)
    ]
    dq_same, dq_pair = pl.pallas_call(
        functools.partial(query_sum_kernel, chips),
        out_shape=(shape(2, rows, LANES),) * 2,
        in_specs=[VMEM] * chips,
        out_specs=(VMEM,) * 2,
        compiler_params=SMALL,
        name="query_sum",
    )(*dq)
    dq_pair = send(dq_pair, "row", row_count, 1)
    dkv_own, dkv_sibling = pl.pallas_call(
        functools.partial(key_sum_kernel, row_count),
        out_shape=(kv_shape,) * 2,
        in_specs=[VMEM] * row_count,
        out_specs=(VMEM,) * 2,
        compiler_params=SMALL,
        cost_estimate=early(20),
        name="key_sum",
    )(*dkv)
    to_sibling = pl.pallas_call(
        bundle_kernel,
        out_shape=shape(2, 2 * krows + rows, LANES),
        in_specs=[VMEM] * 3,
        out_specs=VMEM,
        compiler_params=SMALL,
        name="bundle",
    )(dkv_sibling, dq_same, dq_pair)
    from_sibling = send(to_sibling, "core", cores, 1)
    return pl.pallas_call(
        functools.partial(finish_kernel, krows),
        out_shape=(shape(1, rows, width), shape(1, krows, width), shape(1, krows, width)),
        in_specs=[VMEM] * 4,
        out_specs=(VMEM,) * 3,
        compiler_params=SMALL,
        name="finish",
    )(dkv_own, dq_same, dq_pair, from_sibling)


def solution(mesh):
    row_count, columns = mesh.devices.shape
    cores = 2
    chips = columns // cores
    fine = Mesh(mesh.devices.reshape(row_count, chips, cores), ("row", "chip", "core"))
    col = ("chip", "core")
    in_specs = (
        P("row", col, None),
        P(col, "row", None),
        P(col, "row", None),
        P("row", col, None),
        P("row", col, None),
        P("row", None, None),
        P("row", col, None),
        P("row", col),
        P("row", col, None, None, None),
    )
    out_specs = (P("row", col, None), P(col, "row", None), P(col, "row", None))
    return jax.shard_map(
        functools.partial(body, (row_count, chips, cores)),
        mesh=fine, in_specs=in_specs, out_specs=out_specs, check_vma=False,
    )
```

profile of v0, /device:TPU:0, one launch (start us, length us, event | category | flops | bytes accessed | tf_op | source)
XLA Modules:
  0.0 56.8 jit_solution(4464431069276656336)
XLA Ops:
  0.6 0.0 copy-start.2
  1.3 0.0 copy-done.2
  1.3 0.0 copy-start.1
  1.3 0.7 %copy-done.1 = f32[1,8,1024]{2,1,0:T(8,128)S(1)} copy-done((f32[1,8,1024]{2,1,0:T(8,128)S(1)}, f32[1,8,1024]{2,1,0:T(8,128)}, u32[]{:S(2)}) %copy-start.1) | copy-done | bytes 32792
  2.1 2.4 %pack.1 = (bf16[272,128]{1,0:T(8,128)(2,1)S(1)}, bf16[272,128]{1,0:T(8,128)(2,1)S(1)}, bf16[272,128]{1,0:T(8,128)(2,1)S(1)}, bf16[512,128]{1,0:T(8,128)(2,1)}, b...) custom-call(bf16[1,128,512]{2,1,0:T(8,128)(2,1)} %q_hbm.1, ...), custom_call_target="tpu_custom_call" | custom-call | tf_op jit(solution)/shard_map/pack/pallas_call | solution.py:376
  4.4 0.5 collective-permute-start
  5.0 2.7 %collective-permute-start.1 = (bf16[272,128]{1,0:T(8,128)(2,1)S(1)}, bf16[272,128]{1,0:T(8,128)(2,1)S(1)}, u32[]{:S(2)}, u32[]{:S(2)}) collective-permute-start(bf16[272,128]{1,0:T(8,128)(2,1)S(1)} %get-tuple-element.35), channel_id=1, source_target_pairs={{0,8},{1,9},{8,0},{9,1},{16,24},{17,25},{24,16},{25,17},{2,10},{3,... | collective-permute-start | bytes 208904 | tf_op jit(solution)/shard_map/ppermute | solution.py:353
  7.6 0.1 collective-permute-start.2
  7.7 1.7 %collective-permute-start.3 = (s32[15,8,128]{2,1,0:T(8,128)S(1)}, s32[15,8,128]{2,1,0:T(8,128)S(1)}, u32[]{:S(2)}, u32[]{:S(2)}) collective-permute-start(s32[15,8,128]{2,1,0:T(8,128)S(1)} %get-tuple-element.37.bits_own), channel_id=1, source_target_pairs={{0,8},{8,0},{16,24},{24,16},{1,9},{9,1},{17,25},{25,17},{2,10},{10... | collective-permute-start | bytes 184328 | tf_op jit(solution)/shard_map/ppermute | solution.py:353
  9.4 0.0 collective-permute-done.sib_ref
  9.4 0.0 copy-start
  9.4 0.9 %copy-done = bf16[512,128]{1,0:T(8,128)(2,1)S(1)} copy-done((bf16[512,128]{1,0:T(8,128)(2,1)S(1)}, bf16[512,128]{1,0:T(8,128)(2,1)}, u32[]{:S(2)}) %copy-start) | copy-done | bytes 131096
  10.4 2.7 %collective-permute-start.7 = (bf16[2,256,128]{2,1,0:T(8,128)(2,1)S(1)}, bf16[2,256,128]{2,1,0:T(8,128)(2,1)S(1)}, u32[]{:S(2)}, u32[]{:S(2)}) collective-permute-start(bf16[2,256,128]{2,1,0:T(8,128)(2,1)S(1)} %get-tuple-element.41.same_ref), channel_id=1, source_target_pairs={{0,16},{8,24},{16,0},{24,8},{1,17},{9,25},{17,1},{25,9},{2,18},{10... | collective-permute-start | bytes 393224 | tf_op jit(solution)/shard_map/ppermute | solution.py:353
  13.0 0.1 collective-permute-start.8
  13.1 0.3 collective-permute-done.3.bits_pair
  13.4 0.0 collective-permute-done.1.pair0_ref
  13.4 0.0 collective-permute-done.2.pair1_ref
  13.5 2.5 %collective-permute-start.6 = (bf16[4,272,128]{2,1,0:T(8,128)(2,1)S(1)}, bf16[4,272,128]{2,1,0:T(8,128)(2,1)S(1)}, u32[]{:S(2)}, u32[]{:S(2)}) collective-permute-start(bf16[4,272,128]{2,1,0:T(8,128)(2,1)S(1)} %get-tuple-element.39.refs_0_), channel_id=1, source_target_pairs={{0,6},{2,4},{4,2},{6,0},{1,7},{3,5},{5,3},{7,1},{8,14},{10,12},{12... | collective-permute-start | bytes 835592 | tf_op jit(solution)/shard_map/ppermute | solution.py:353
  16.0 0.5 collective-permute-start.5
  16.5 0.5 collective-permute-start.4
  17.0 6.3 %collective-permute-done.7.refs_0_ = bf16[2,256,128]{2,1,0:T(8,128)(2,1)S(1)} collective-permute-done((bf16[2,256,128]{2,1,0:T(8,128)(2,1)S(1)}, bf16[2,256,128]{2,1,0:T(8,128)(2,1)S(1)}, u32[]{:S(2)}, u32[]{:S(2)}) %collective-permute-start.7) | collective-permute-done | bytes 131104 | tf_op jit(solution)/shard_map/ppermute | solution.py:353
  23.3 0.0 collective-permute-done.8.refs_1_
  23.3 2.5 %collective-permute-start.9 = (bf16[2,256,128]{2,1,0:T(8,128)(2,1)S(1)}, bf16[2,256,128]{2,1,0:T(8,128)(2,1)S(1)}, u32[]{:S(2)}, u32[]{:S(2)}) collective-permute-start(bf16[2,256,128]{2,1,0:T(8,128)(2,1)S(1)} %get-tuple-element.43), channel_id=1, source_target_pairs={{0,8},{8,0},{16,24},{24,16},{1,9},{9,1},{17,25},{25,17},{2,10},{10... | collective-permute-start | bytes 393224 | tf_op jit(solution)/shard_map/ppermute | solution.py:353
  25.9 0.0 collective-permute-start.10
  25.9 2.9 %collective-permute-done.9.pair_ref = bf16[2,256,128]{2,1,0:T(8,128)(2,1)S(1)} collective-permute-done((bf16[2,256,128]{2,1,0:T(8,128)(2,1)S(1)}, bf16[2,256,128]{2,1,0:T(8,128)(2,1)S(1)}, u32[]{:S(2)}, u32[]{:S(2)}) %collective-permute-start.9) | collective-permute-done | bytes 131104 | tf_op jit(solution)/shard_map/ppermute | solution.py:353
  28.8 0.2 key_place.1
  29.0 0.0 collective-permute-done.10.refs_8_
  29.0 0.0 collective-permute-done.6.refs_3_
  29.0 0.0 collective-permute-done.5.refs_2_
  29.0 0.0 collective-permute-done.4.refs_1_
  29.0 6.7 %pair.1 = (bf16[2,8,128,128]{3,2,1,0:T(8,128)(2,1)S(1)}, bf16[2,256,128]{2,1,0:T(8,128)(2,1)S(1)}, bf16[2,256,128]{2,1,0:T(8,128)(2,1)S(1)}, bf16[2,256,128]{2,1,0:T(8,128)(2,1)S(1)}, bf16[2,256,128]{2,1,0:T(8,128)(2,1)S(1)}) custom-call(bf16[4,272,128]{2,1,0:T(8,128)(2,1)S(1)} %get-tuple-element.39.refs_0_, ...), custom_call_target="tpu_custom_call" | custom-call | tf_op jit(solution)/shard_map/pair/pallas_call | solution.py:451
  35.7 0.2 turn.1
  36.0 1.6 %collective-permute-start.14 = (bf16[4,128,128]{2,1,0:T(8,128)(2,1)S(1)}, bf16[4,128,128]{2,1,0:T(8,128)(2,1)S(1)}, u32[]{:S(2)}, u32[]{:S(2)}) collective-permute-start(bf16[4,128,128]{2,1,0:T(8,128)(2,1)S(1)} %get-tuple-element.57), channel_id=1, source_target_pairs={{0,2},{2,0},{4,6},{6,4},{1,3},{3,1},{5,7},{7,5},{8,10},{10,8},{12,... | collective-permute-start | bytes 393224 | tf_op jit(solution)/shard_map/ppermute | solution.py:353
  37.5 3.7 %collective-permute-start.15 = (bf16[4,128,128]{2,1,0:T(8,128)(2,1)S(1)}, bf16[4,128,128]{2,1,0:T(8,128)(2,1)S(1)}, u32[]{:S(2)}, u32[]{:S(2)}) collective-permute-start(bf16[4,128,128]{2,1,0:T(8,128)(2,1)S(1)} %get-tuple-element.58), channel_id=1, source_target_pairs={{0,4},{2,6},{4,0},{6,2},{1,5},{3,7},{5,1},{7,3},{8,12},{10,14},{12... | collective-permute-start | bytes 393224 | tf_op jit(solution)/shard_map/ppermute | solution.py:353
  41.3 0.0 collective-permute-start.16
  41.3 2.0 %collective-permute-start.11 = (bf16[2,256,128]{2,1,0:T(8,128)(2,1)S(1)}, bf16[2,256,128]{2,1,0:T(8,128)(2,1)S(1)}, u32[]{:S(2)}, u32[]{:S(2)}) collective-permute-start(bf16[2,256,128]{2,1,0:T(8,128)(2,1)S(1)} %get-tuple-element.51), channel_id=1, source_target_pairs={{0,24},{8,16},{16,8},{24,0},{1,25},{9,17},{17,9},{25,1},{2,26},{10... | collective-permute-start | bytes 393224 | tf_op jit(solution)/shard_map/ppermute | solution.py:353
  43.3 1.4 %collective-permute-start.12 = (bf16[2,256,128]{2,1,0:T(8,128)(2,1)S(1)}, bf16[2,256,128]{2,1,0:T(8,128)(2,1)S(1)}, u32[]{:S(2)}, u32[]{:S(2)}) collective-permute-start(bf16[2,256,128]{2,1,0:T(8,128)(2,1)S(1)} %get-tuple-element.52), channel_id=1, source_target_pairs={{0,16},{8,24},{16,0},{24,8},{1,17},{9,25},{17,1},{25,9},{2,18},{10... | collective-permute-start | bytes 393224 | tf_op jit(solution)/shard_map/ppermute | solution.py:353
  44.7 0.0 collective-permute-done.14.refs_1_
  44.7 0.9 %collective-permute-start.13 = (bf16[2,256,128]{2,1,0:T(8,128)(2,1)S(1)}, bf16[2,256,128]{2,1,0:T(8,128)(2,1)S(1)}, u32[]{:S(2)}, u32[]{:S(2)}) collective-permute-start(bf16[2,256,128]{2,1,0:T(8,128)(2,1)S(1)} %get-tuple-element.53), channel_id=1, source_target_pairs={{0,8},{8,0},{16,24},{24,16},{1,9},{9,1},{17,25},{25,17},{2,10},{10... | collective-permute-start | bytes 393224 | tf_op jit(solution)/shard_map/ppermute | solution.py:353
  45.6 0.0 collective-permute-done.15.refs_2_
  45.7 1.5 %collective-permute-done.16.refs_3_ = bf16[4,128,128]{2,1,0:T(8,128)(2,1)S(1)} collective-permute-done((bf16[4,128,128]{2,1,0:T(8,128)(2,1)S(1)}, bf16[4,128,128]{2,1,0:T(8,128)(2,1)S(1)}, u32[]{:S(2)}, u32[]{:S(2)}) %collective-permute-start.16) | collective-permute-done | bytes 131104 | tf_op jit(solution)/shard_map/ppermute | solution.py:353
  47.1 0.1 query_sum.1
  47.2 2.1 %collective-permute-start.17 = (bf16[2,128,128]{2,1,0:T(8,128)(2,1)S(1)}, bf16[2,128,128]{2,1,0:T(8,128)(2,1)S(1)}, u32[]{:S(2)}, u32[]{:S(2)}) collective-permute-start(bf16[2,128,128]{2,1,0:T(8,128)(2,1)S(1)} %get-tuple-element.61), channel_id=1, source_target_pairs={{0,8},{8,0},{16,24},{24,16},{1,9},{9,1},{17,25},{25,17},{2,10},{10... | collective-permute-start | bytes 196616 | tf_op jit(solution)/shard_map/ppermute | solution.py:353
  49.3 0.0 collective-permute-done.11.refs_1_
  49.3 5.1 %collective-permute-done.12.refs_2_ = bf16[2,256,128]{2,1,0:T(8,128)(2,1)S(1)} collective-permute-done((bf16[2,256,128]{2,1,0:T(8,128)(2,1)S(1)}, bf16[2,256,128]{2,1,0:T(8,128)(2,1)S(1)}, u32[]{:S(2)}, u32[]{:S(2)}) %collective-permute-start.12) | collective-permute-done | bytes 131104 | tf_op jit(solution)/shard_map/ppermute | solution.py:353
  54.4 0.0 collective-permute-done.13.refs_3_
  54.4 0.1 key_sum.1
  54.4 0.0 collective-permute-done.17.dq_pair
  54.5 0.1 collective-permute-start.18
  54.5 1.4 %collective-permute-done.18.sib_ref = bf16[2,384,128]{2,1,0:T(8,128)(2,1)S(1)} collective-permute-done((bf16[2,384,128]{2,1,0:T(8,128)(2,1)S(1)}, bf16[2,384,128]{2,1,0:T(8,128)(2,1)S(1)}, u32[]{:S(2)}, u32[]{:S(2)}) %collective-permute-start.18) | collective-permute-done | bytes 196640 | tf_op jit(solution)/shard_map/ppermute | solution.py:353
  56.0 0.8 %finish.1 = (bf16[1,128,512]{2,1,0:T(8,128)(2,1)}, bf16[1,128,512]{2,1,0:T(8,128)(2,1)}, bf16[1,128,512]{2,1,0:T(8,128)(2,1)}) custom-call(bf16[2,256,128]{2,1,0:T(8,128)(2,1)S(1)} %get-tuple-element.54.dkv_own, bf16[2,128,128]{2,1,0:T(8,128)(2,1)S(1)} %get-tuple-element.60.dq_same, bf16[2,128,128]{2,1,0:T(8,128)(2,1)S(1)} %collective-permute-done.17.dq_pair, ...), custom_call_target="tpu_custom_call" | custom-call | tf_op jit(solution)/shard_map/finish/pallas_call | solution.py:513
  (4 shorter events, 0.1 us)
Async XLA Ops:
  0.6 0.7 %copy-start.2 = (s32[1,1,24]{2,1,0:T(1,128)S(1)}, s32[1,1,24]{2,1,0:T(1,128)}, u32[]{:S(2)}) copy-start(s32[1,1,24]{2,1,0:T(1,128)} %slot_ref.1) | copy-start | bytes 292
  1.3 0.8 %copy-start.1 = (f32[1,8,1024]{2,1,0:T(8,128)S(1)}, f32[1,8,1024]{2,1,0:T(8,128)}, u32[]{:S(2)}) copy-start(f32[1,8,1024]{2,1,0:T(8,128)} %lse_hbm.1) | copy-start | bytes 98308
  4.4 5.0 %collective-permute-start = (bf16[784,128]{1,0:T(8,128)(2,1)}, bf16[784,128]{1,0:T(8,128)(2,1)S(1)}, u32[]{:S(2)}, u32[]{:S(2)}) collective-permute-start(bf16[784,128]{1,0:T(8,128)(2,1)} %get-tuple-element.34), channel_id=1, source_target_pairs={{0,1},{1,0},{2,3},{3,2},{4,5},{5,4},{6,7},{7,6},{8,9},{9,8},{10,11... | collective-permute-start | bytes 602120 | tf_op jit(solution)/shard_map/ppermute | solution.py:353
  5.0 8.5 %collective-permute-start.1 = (bf16[272,128]{1,0:T(8,128)(2,1)S(1)}, bf16[272,128]{1,0:T(8,128)(2,1)S(1)}, u32[]{:S(2)}, u32[]{:S(2)}) collective-permute-start(bf16[272,128]{1,0:T(8,128)(2,1)S(1)} %get-tuple-element.35), channel_id=1, source_target_pairs={{0,8},{1,9},{8,0},{9,1},{16,24},{17,25},{24,16},{25,17},{2,10},{3,... | collective-permute-start | bytes 208904 | tf_op jit(solution)/shard_map/ppermute | solution.py:353
  7.6 5.8 %collective-permute-start.2 = (bf16[272,128]{1,0:T(8,128)(2,1)S(1)}, bf16[272,128]{1,0:T(8,128)(2,1)S(1)}, u32[]{:S(2)}, u32[]{:S(2)}) collective-permute-start(bf16[272,128]{1,0:T(8,128)(2,1)S(1)} %get-tuple-element.36), channel_id=1, source_target_pairs={{0,9},{1,8},{8,1},{9,0},{16,25},{17,24},{24,17},{25,16},{2,11},{3,... | collective-permute-start | bytes 208904 | tf_op jit(solution)/shard_map/ppermute | solution.py:353
  7.7 5.7 %collective-permute-start.3 = (s32[15,8,128]{2,1,0:T(8,128)S(1)}, s32[15,8,128]{2,1,0:T(8,128)S(1)}, u32[]{:S(2)}, u32[]{:S(2)}) collective-permute-start(s32[15,8,128]{2,1,0:T(8,128)S(1)} %get-tuple-element.37.bits_own), channel_id=1, source_target_pairs={{0,8},{8,0},{16,24},{24,16},{1,9},{9,1},{17,25},{25,17},{2,10},{10... | collective-permute-start | bytes 184328 | tf_op jit(solution)/shard_map/ppermute | solution.py:353
  9.4 0.9 %copy-start = (bf16[512,128]{1,0:T(8,128)(2,1)S(1)}, bf16[512,128]{1,0:T(8,128)(2,1)}, u32[]{:S(2)}) copy-start(bf16[512,128]{1,0:T(8,128)(2,1)} %get-tuple-element.40.kv_own) | copy-start | bytes 393220
  10.4 12.9 %collective-permute-start.7 = (bf16[2,256,128]{2,1,0:T(8,128)(2,1)S(1)}, bf16[2,256,128]{2,1,0:T(8,128)(2,1)S(1)}, u32[]{:S(2)}, u32[]{:S(2)}) collective-permute-start(bf16[2,256,128]{2,1,0:T(8,128)(2,1)S(1)} %get-tuple-element.41.same_ref), channel_id=1, source_target_pairs={{0,16},{8,24},{16,0},{24,8},{1,17},{9,25},{17,1},{25,9},{2,18},{10... | collective-permute-start | bytes 393224 | tf_op jit(solution)/shard_map/ppermute | solution.py:353
  13.0 10.3 %collective-permute-start.8 = (bf16[2,256,128]{2,1,0:T(8,128)(2,1)S(1)}, bf16[2,256,128]{2,1,0:T(8,128)(2,1)S(1)}, u32[]{:S(2)}, u32[]{:S(2)}) collective-permute-start(bf16[2,256,128]{2,1,0:T(8,128)(2,1)S(1)} %get-tuple-element.42.pair_ref), channel_id=1, source_target_pairs={{0,24},{8,16},{16,8},{24,0},{1,25},{9,17},{17,9},{25,1},{2,26},{10... | collective-permute-start | bytes 393224 | tf_op jit(solution)/shard_map/ppermute | solution.py:353
  13.5 15.5 %collective-permute-start.6 = (bf16[4,272,128]{2,1,0:T(8,128)(2,1)S(1)}, bf16[4,272,128]{2,1,0:T(8,128)(2,1)S(1)}, u32[]{:S(2)}, u32[]{:S(2)}) collective-permute-start(bf16[4,272,128]{2,1,0:T(8,128)(2,1)S(1)} %get-tuple-element.39.refs_0_), channel_id=1, source_target_pairs={{0,6},{2,4},{4,2},{6,0},{1,7},{3,5},{5,3},{7,1},{8,14},{10,12},{12... | collective-permute-start | bytes 835592 | tf_op jit(solution)/shard_map/ppermute | solution.py:353
  16.0 13.0 %collective-permute-start.5 = (bf16[4,272,128]{2,1,0:T(8,128)(2,1)S(1)}, bf16[4,272,128]{2,1,0:T(8,128)(2,1)S(1)}, u32[]{:S(2)}, u32[]{:S(2)}) collective-permute-start(bf16[4,272,128]{2,1,0:T(8,128)(2,1)S(1)} %get-tuple-element.39.refs_0_), channel_id=1, source_target_pairs={{0,4},{2,6},{4,0},{6,2},{1,5},{3,7},{5,1},{7,3},{8,12},{10,14},{12... | collective-permute-start | bytes 835592 | tf_op jit(solution)/shard_map/ppermute | solution.py:353
  16.5 12.5 %collective-permute-start.4 = (bf16[4,272,128]{2,1,0:T(8,128)(2,1)S(1)}, bf16[4,272,128]{2,1,0:T(8,128)(2,1)S(1)}, u32[]{:S(2)}, u32[]{:S(2)}) collective-permute-start(bf16[4,272,128]{2,1,0:T(8,128)(2,1)S(1)} %get-tuple-element.39.refs_0_), channel_id=1, source_target_pairs={{0,2},{2,0},{4,6},{6,4},{1,3},{3,1},{5,7},{7,5},{8,10},{10,8},{12,... | collective-permute-start | bytes 835592 | tf_op jit(solution)/shard_map/ppermute | solution.py:353
  23.3 5.5 %collective-permute-start.9 = (bf16[2,256,128]{2,1,0:T(8,128)(2,1)S(1)}, bf16[2,256,128]{2,1,0:T(8,128)(2,1)S(1)}, u32[]{:S(2)}, u32[]{:S(2)}) collective-permute-start(bf16[2,256,128]{2,1,0:T(8,128)(2,1)S(1)} %get-tuple-element.43), channel_id=1, source_target_pairs={{0,8},{8,0},{16,24},{24,16},{1,9},{9,1},{17,25},{25,17},{2,10},{10... | collective-permute-start | bytes 393224 | tf_op jit(solution)/shard_map/ppermute | solution.py:353
  25.9 3.1 %collective-permute-start.10 = (s32[2,13,8,128]{3,2,1,0:T(8,128)S(1)}, s32[2,13,8,128]{3,2,1,0:T(8,128)S(1)}, u32[]{:S(2)}, u32[]{:S(2)}) collective-permute-start(s32[2,13,8,128]{3,2,1,0:T(8,128)S(1)} %get-tuple-element.48.refs_7_), channel_id=1, source_target_pairs={{0,1},{1,0},{2,3},{3,2},{4,5},{5,4},{6,7},{7,6},{8,9},{9,8},{10,11... | collective-permute-start | bytes 319496 | tf_op jit(solution)/shard_map/ppermute | solution.py:353
  36.0 8.8 %collective-permute-start.14 = (bf16[4,128,128]{2,1,0:T(8,128)(2,1)S(1)}, bf16[4,128,128]{2,1,0:T(8,128)(2,1)S(1)}, u32[]{:S(2)}, u32[]{:S(2)}) collective-permute-start(bf16[4,128,128]{2,1,0:T(8,128)(2,1)S(1)} %get-tuple-element.57), channel_id=1, source_target_pairs={{0,2},{2,0},{4,6},{6,4},{1,3},{3,1},{5,7},{7,5},{8,10},{10,8},{12,... | collective-permute-start | bytes 393224 | tf_op jit(solution)/shard_map/ppermute | solution.py:353
  37.5 8.1 %collective-permute-start.15 = (bf16[4,128,128]{2,1,0:T(8,128)(2,1)S(1)}, bf16[4,128,128]{2,1,0:T(8,128)(2,1)S(1)}, u32[]{:S(2)}, u32[]{:S(2)}) collective-permute-start(bf16[4,128,128]{2,1,0:T(8,128)(2,1)S(1)} %get-tuple-element.58), channel_id=1, source_target_pairs={{0,4},{2,6},{4,0},{6,2},{1,5},{3,7},{5,1},{7,3},{8,12},{10,14},{12... | collective-permute-start | bytes 393224 | tf_op jit(solution)/shard_map/ppermute | solution.py:353
  41.3 5.9 %collective-permute-start.16 = (bf16[4,128,128]{2,1,0:T(8,128)(2,1)S(1)}, bf16[4,128,128]{2,1,0:T(8,128)(2,1)S(1)}, u32[]{:S(2)}, u32[]{:S(2)}) collective-permute-start(bf16[4,128,128]{2,1,0:T(8,128)(2,1)S(1)} %get-tuple-element.59), channel_id=1, source_target_pairs={{0,6},{2,4},{4,2},{6,0},{1,7},{3,5},{5,3},{7,1},{8,14},{10,12},{12... | collective-permute-start | bytes 393224 | tf_op jit(solution)/shard_map/ppermute | solution.py:353
  41.3 8.0 %collective-permute-start.11 = (bf16[2,256,128]{2,1,0:T(8,128)(2,1)S(1)}, bf16[2,256,128]{2,1,0:T(8,128)(2,1)S(1)}, u32[]{:S(2)}, u32[]{:S(2)}) collective-permute-start(bf16[2,256,128]{2,1,0:T(8,128)(2,1)S(1)} %get-tuple-element.51), channel_id=1, source_target_pairs={{0,24},{8,16},{16,8},{24,0},{1,25},{9,17},{17,9},{25,1},{2,26},{10... | collective-permute-start | bytes 393224 | tf_op jit(solution)/shard_map/ppermute | solution.py:353
  43.3 11.1 %collective-permute-start.12 = (bf16[2,256,128]{2,1,0:T(8,128)(2,1)S(1)}, bf16[2,256,128]{2,1,0:T(8,128)(2,1)S(1)}, u32[]{:S(2)}, u32[]{:S(2)}) collective-permute-start(bf16[2,256,128]{2,1,0:T(8,128)(2,1)S(1)} %get-tuple-element.52), channel_id=1, source_target_pairs={{0,16},{8,24},{16,0},{24,8},{1,17},{9,25},{17,1},{25,9},{2,18},{10... | collective-permute-start | bytes 393224 | tf_op jit(solution)/shard_map/ppermute | solution.py:353
  44.7 9.6 %collective-permute-start.13 = (bf16[2,256,128]{2,1,0:T(8,128)(2,1)S(1)}, bf16[2,256,128]{2,1,0:T(8,128)(2,1)S(1)}, u32[]{:S(2)}, u32[]{:S(2)}) collective-permute-start(bf16[2,256,128]{2,1,0:T(8,128)(2,1)S(1)} %get-tuple-element.53), channel_id=1, source_target_pairs={{0,8},{8,0},{16,24},{24,16},{1,9},{9,1},{17,25},{25,17},{2,10},{10... | collective-permute-start | bytes 393224 | tf_op jit(solution)/shard_map/ppermute | solution.py:353
  47.2 7.2 %collective-permute-start.17 = (bf16[2,128,128]{2,1,0:T(8,128)(2,1)S(1)}, bf16[2,128,128]{2,1,0:T(8,128)(2,1)S(1)}, u32[]{:S(2)}, u32[]{:S(2)}) collective-permute-start(bf16[2,128,128]{2,1,0:T(8,128)(2,1)S(1)} %get-tuple-element.61), channel_id=1, source_target_pairs={{0,8},{8,0},{16,24},{24,16},{1,9},{9,1},{17,25},{25,17},{2,10},{10... | collective-permute-start | bytes 196616 | tf_op jit(solution)/shard_map/ppermute | solution.py:353
  54.5 1.5 %collective-permute-start.18 = (bf16[2,384,128]{2,1,0:T(8,128)(2,1)S(1)}, bf16[2,384,128]{2,1,0:T(8,128)(2,1)S(1)}, u32[]{:S(2)}, u32[]{:S(2)}) collective-permute-start(bf16[2,384,128]{2,1,0:T(8,128)(2,1)S(1)} %bundle.1), channel_id=1, source_target_pairs={{0,1},{1,0},{2,3},{3,2},{4,5},{5,4},{6,7},{7,6},{8,9},{9,8},{10,11... | collective-permute-start | bytes 589832 | tf_op jit(solution)/shard_map/ppermute | solution.py:353
where the time goes:
time: 57.4 us; the launch traced here: 56.8 us
  starting transfers between devices  25.6 us (45%)
  waiting for transfers between devices  17.6 us (31%)
  Pallas kernels  10.5 us (18%)
  local copies, waits for them, and re-layouts  1.66 us (3%)
  between operations  1.44 us (3%)
    ppermute x19, starting transfers between devices, send(): lax.ppermute(block, axes, [(place, place ^ step) for place in range(count)])  25.6 us
    ppermute x19, waiting for transfers between devices, send(): lax.ppermute(block, axes, [(place, place ^ step) for place in range(count)])  17.6 us
    pallas_call x1, Pallas kernels, body(): pl.pallas_call(functools.partial(pair_kernel, (head_dim, tile, capacity,...  6.69 us
    pallas_call x1, Pallas kernels, body(): pl.pallas_call(functools.partial(pack_kernel, heads), out_shape=(qg_shape...  2.37 us
    unnamed x6, local copies, waits for them, and re-layouts  1.66 us
  transfers between devices with their start and end apart: 19, of which 6 were waited for; matrix products, arithmetic and copies ran while one was open for 0% of the time, Pallas kernels for 1%

commit v1 on v0

--- a/solution.py
+++ b/solution.py
@@ -479,7 +479,7 @@
         compiler_params=SMALL,
         name="turn",
     )(parts[0])
-    dq = [dq[0]] + [send(dq[step], "chip", chips, step) for step in range(1, chips)]
+    dq = [dq[0]] + [send(dq[step], "chip", chips, step) for step in range(chips - 1, 0, -1)]
     dkv = [dkv[0]] + [
         send(dkv[step], "row", row_count, step) for step in range(row_count - 1, 0, -1)
     ]

time: 57.4 us -> 58.1 us (1.012)
  starting transfers between devices: 25.6 us -> 27.2 us
  Pallas kernels: 10.5 us -> 9.42 us
  waiting for transfers between devices: 17.6 us -> 18.2 us
    ppermute x19, starting transfers between devices: 25.6 us -> 27.2 us  [send(): lax.ppermute(block, axes, [(place, place ^ step) for place in range(count)])]
    pallas_call x1, Pallas kernels: 6.69 us -> 5.6 us  [body(): pl.pallas_call(functools.partial(pair_kernel, (head_dim, tile, capacity,...]
    ppermute x19, waiting for transfers between devices: 17.6 us -> 18.2 us  [send(): lax.ppermute(block, axes, [(place, place ^ step) for place in range(count)])]
  transfers between devices with their start and end apart: 19 -> 19, of which waited for: 6 -> 7; matrix products, arithmetic and copies ran while one was open for 0% -> 0% of each run, Pallas kernels for 1% -> 1%
where the time goes in v1:
time: 58.1 us; the launch traced here: 57.9 us
  starting transfers between devices  27.2 us (47%)
  waiting for transfers between devices  18.2 us (31%)
  Pallas kernels  9.42 us (16%)
  local copies, waits for them, and re-layouts  1.66 us (3%)
  between operations  1.44 us (2%)
    ppermute x19, starting transfers between devices, send(): lax.ppermute(block, axes, [(place, place ^ step) for place in range(count)])  27.2 us
    ppermute x19, waiting for transfers between devices, send(): lax.ppermute(block, axes, [(place, place ^ step) for place in range(count)])  18.2 us
    pallas_call x1, Pallas kernels, body(): pl.pallas_call(functools.partial(pair_kernel, (head_dim, tile, capacity,...  5.6 us
    pallas_call x1, Pallas kernels, body(): pl.pallas_call(functools.partial(pack_kernel, heads), out_shape=(qg_shape...  2.37 us
    unnamed x6, local copies, waits for them, and re-layouts  1.66 us
  transfers between devices with their start and end apart: 19, of which 7 were waited for; matrix products, arithmetic and copies ran while one was open for 0% of the time, Pallas kernels for 1%

profile of v1, /device:TPU:0, one launch (start us, length us, event | category | flops | bytes accessed | tf_op | source)
XLA Modules:
  0.0 57.9 jit_solution(6687069450348650954)
XLA Ops:
  0.6 0.0 copy-start.2
  1.3 0.0 copy-done.2
  1.3 0.0 copy-start.1
  1.3 0.7 %copy-done.1 = f32[1,8,1024]{2,1,0:T(8,128)S(1)} copy-done((f32[1,8,1024]{2,1,0:T(8,128)S(1)}, f32[1,8,1024]{2,1,0:T(8,128)}, u32[]{:S(2)}) %copy-start.1) | copy-done | bytes 32792
  2.1 2.4 %pack.1 = (bf16[272,128]{1,0:T(8,128)(2,1)S(1)}, bf16[272,128]{1,0:T(8,128)(2,1)S(1)}, bf16[272,128]{1,0:T(8,128)(2,1)S(1)}, bf16[512,128]{1,0:T(8,128)(2,1)}, b...) custom-call(bf16[1,128,512]{2,1,0:T(8,128)(2,1)} %q_hbm.1, ...), custom_call_target="tpu_custom_call" | custom-call | tf_op jit(solution)/shard_map/pack/pallas_call | solution.py:376
  4.4 0.5 collective-permute-start
  5.0 2.7 %collective-permute-start.1 = (bf16[272,128]{1,0:T(8,128)(2,1)S(1)}, bf16[272,128]{1,0:T(8,128)(2,1)S(1)}, u32[]{:S(2)}, u32[]{:S(2)}) collective-permute-start(bf16[272,128]{1,0:T(8,128)(2,1)S(1)} %get-tuple-element.35), channel_id=1, source_target_pairs={{0,8},{1,9},{8,0},{9,1},{16,24},{17,25},{24,16},{25,17},{2,10},{3,... | collective-permute-start | bytes 208904 | tf_op jit(solution)/shard_map/ppermute | solution.py:353
  7.6 0.1 collective-permute-start.2
  7.7 1.7 %collective-permute-start.3 = (s32[15,8,128]{2,1,0:T(8,128)S(1)}, s32[15,8,128]{2,1,0:T(8,128)S(1)}, u32[]{:S(2)}, u32[]{:S(2)}) collective-permute-start(s32[15,8,128]{2,1,0:T(8,128)S(1)} %get-tuple-element.37.bits_own), channel_id=1, source_target_pairs={{0,8},{8,0},{16,24},{24,16},{1,9},{9,1},{17,25},{25,17},{2,10},{10... | collective-permute-start | bytes 184328 | tf_op jit(solution)/shard_map/ppermute | solution.py:353
  9.4 0.0 collective-permute-done.sib_ref
  9.4 0.0 copy-start
  9.4 0.9 %copy-done = bf16[512,128]{1,0:T(8,128)(2,1)S(1)} copy-done((bf16[512,128]{1,0:T(8,128)(2,1)S(1)}, bf16[512,128]{1,0:T(8,128)(2,1)}, u32[]{:S(2)}) %copy-start) | copy-done | bytes 131096
  10.4 2.7 %collective-permute-start.7 = (bf16[2,256,128]{2,1,0:T(8,128)(2,1)S(1)}, bf16[2,256,128]{2,1,0:T(8,128)(2,1)S(1)}, u32[]{:S(2)}, u32[]{:S(2)}) collective-permute-start(bf16[2,256,128]{2,1,0:T(8,128)(2,1)S(1)} %get-tuple-element.41.same_ref), channel_id=1, source_target_pairs={{0,16},{8,24},{16,0},{24,8},{1,17},{9,25},{17,1},{25,9},{2,18},{10... | collective-permute-start | bytes 393224 | tf_op jit(solution)/shard_map/ppermute | solution.py:353
  13.0 0.1 collective-permute-start.8
  13.1 0.3 collective-permute-done.3.bits_pair
  13.4 0.0 collective-permute-done.1.pair0_ref
  13.4 0.0 collective-permute-done.2.pair1_ref
  13.5 2.5 %collective-permute-start.6 = (bf16[4,272,128]{2,1,0:T(8,128)(2,1)S(1)}, bf16[4,272,128]{2,1,0:T(8,128)(2,1)S(1)}, u32[]{:S(2)}, u32[]{:S(2)}) collective-permute-start(bf16[4,272,128]{2,1,0:T(8,128)(2,1)S(1)} %get-tuple-element.39.refs_0_), channel_id=1, source_target_pairs={{0,6},{2,4},{4,2},{6,0},{1,7},{3,5},{5,3},{7,1},{8,14},{10,12},{12... | collective-permute-start | bytes 835592 | tf_op jit(solution)/shard_map/ppermute | solution.py:353
  16.0 0.5 collective-permute-start.5
  16.5 0.5 collective-permute-start.4
  17.0 6.3 %collective-permute-done.7.refs_0_ = bf16[2,256,128]{2,1,0:T(8,128)(2,1)S(1)} collective-permute-done((bf16[2,256,128]{2,1,0:T(8,128)(2,1)S(1)}, bf16[2,256,128]{2,1,0:T(8,128)(2,1)S(1)}, u32[]{:S(2)}, u32[]{:S(2)}) %collective-permute-start.7) | collective-permute-done | bytes 131104 | tf_op jit(solution)/shard_map/ppermute | solution.py:353
  23.3 0.0 collective-permute-done.8.refs_1_
  23.3 2.5 %collective-permute-start.9 = (bf16[2,256,128]{2,1,0:T(8,128)(2,1)S(1)}, bf16[2,256,128]{2,1,0:T(8,128)(2,1)S(1)}, u32[]{:S(2)}, u32[]{:S(2)}) collective-permute-start(bf16[2,256,128]{2,1,0:T(8,128)(2,1)S(1)} %get-tuple-element.43), channel_id=1, source_target_pairs={{0,8},{8,0},{16,24},{24,16},{1,9},{9,1},{17,25},{25,17},{2,10},{10... | collective-permute-start | bytes 393224 | tf_op jit(solution)/shard_map/ppermute | solution.py:353
  25.9 0.0 collective-permute-start.10
  25.9 2.9 %collective-permute-done.9.pair_ref = bf16[2,256,128]{2,1,0:T(8,128)(2,1)S(1)} collective-permute-done((bf16[2,256,128]{2,1,0:T(8,128)(2,1)S(1)}, bf16[2,256,128]{2,1,0:T(8,128)(2,1)S(1)}, u32[]{:S(2)}, u32[]{:S(2)}) %collective-permute-start.9) | collective-permute-done | bytes 131104 | tf_op jit(solution)/shard_map/ppermute | solution.py:353
  28.8 0.2 key_place.1
  29.0 0.0 collective-permute-done.10.refs_8_
  29.0 0.0 collective-permute-done.6.refs_3_
  29.0 0.0 collective-permute-done.5.refs_2_
  29.0 0.0 collective-permute-done.4.refs_1_
  29.0 5.6 %pair.1 = (bf16[2,8,128,128]{3,2,1,0:T(8,128)(2,1)S(1)}, bf16[2,256,128]{2,1,0:T(8,128)(2,1)S(1)}, bf16[2,256,128]{2,1,0:T(8,128)(2,1)S(1)}, bf16[2,256,128]{2,1,0:T(8,128)(2,1)S(1)}, bf16[2,256,128]{2,1,0:T(8,128)(2,1)S(1)}) custom-call(bf16[4,272,128]{2,1,0:T(8,128)(2,1)S(1)} %get-tuple-element.39.refs_0_, ...), custom_call_target="tpu_custom_call" | custom-call | tf_op jit(solution)/shard_map/pair/pallas_call | solution.py:451
  34.6 0.2 turn.1
  34.9 1.4 %collective-permute-start.14 = (bf16[4,128,128]{2,1,0:T(8,128)(2,1)S(1)}, bf16[4,128,128]{2,1,0:T(8,128)(2,1)S(1)}, u32[]{:S(2)}, u32[]{:S(2)}) collective-permute-start(bf16[4,128,128]{2,1,0:T(8,128)(2,1)S(1)} %get-tuple-element.57), channel_id=1, source_target_pairs={{0,6},{2,4},{4,2},{6,0},{1,7},{3,5},{5,3},{7,1},{8,14},{10,12},{12... | collective-permute-start | bytes 393224 | tf_op jit(solution)/shard_map/ppermute | solution.py:353
  36.3 4.9 %collective-permute-start.15 = (bf16[4,128,128]{2,1,0:T(8,128)(2,1)S(1)}, bf16[4,128,128]{2,1,0:T(8,128)(2,1)S(1)}, u32[]{:S(2)}, u32[]{:S(2)}) collective-permute-start(bf16[4,128,128]{2,1,0:T(8,128)(2,1)S(1)} %get-tuple-element.58), channel_id=1, source_target_pairs={{0,4},{2,6},{4,0},{6,2},{1,5},{3,7},{5,1},{7,3},{8,12},{10,14},{12... | collective-permute-start | bytes 393224 | tf_op jit(solution)/shard_map/ppermute | solution.py:353
  41.2 0.0 collective-permute-start.16
  41.2 3.8 %collective-permute-start.11 = (bf16[2,256,128]{2,1,0:T(8,128)(2,1)S(1)}, bf16[2,256,128]{2,1,0:T(8,128)(2,1)S(1)}, u32[]{:S(2)}, u32[]{:S(2)}) collective-permute-start(bf16[2,256,128]{2,1,0:T(8,128)(2,1)S(1)} %get-tuple-element.51), channel_id=1, source_target_pairs={{0,24},{8,16},{16,8},{24,0},{1,25},{9,17},{17,9},{25,1},{2,26},{10... | collective-permute-start | bytes 393224 | tf_op jit(solution)/shard_map/ppermute | solution.py:353
  45.0 0.5 collective-permute-start.12
  45.5 0.0 collective-permute-done.14.refs_1_
  45.5 0.6 collective-permute-start.13
  46.1 0.0 collective-permute-done.15.refs_2_
  46.1 0.1 collective-permute-done.16.refs_3_
  46.2 0.1 query_sum.1
  46.2 2.1 %collective-permute-start.17 = (bf16[2,128,128]{2,1,0:T(8,128)(2,1)S(1)}, bf16[2,128,128]{2,1,0:T(8,128)(2,1)S(1)}, u32[]{:S(2)}, u32[]{:S(2)}) collective-permute-start(bf16[2,128,128]{2,1,0:T(8,128)(2,1)S(1)} %get-tuple-element.61), channel_id=1, source_target_pairs={{0,8},{8,0},{16,24},{24,16},{1,9},{9,1},{17,25},{25,17},{2,10},{10... | collective-permute-start | bytes 196616 | tf_op jit(solution)/shard_map/ppermute | solution.py:353
  48.3 1.1 %collective-permute-done.11.refs_1_ = bf16[2,256,128]{2,1,0:T(8,128)(2,1)S(1)} collective-permute-done((bf16[2,256,128]{2,1,0:T(8,128)(2,1)S(1)}, bf16[2,256,128]{2,1,0:T(8,128)(2,1)S(1)}, u32[]{:S(2)}, u32[]{:S(2)}) %collective-permute-start.11) | collective-permute-done | bytes 131104 | tf_op jit(solution)/shard_map/ppermute | solution.py:353
  49.4 6.0 %collective-permute-done.12.refs_2_ = bf16[2,256,128]{2,1,0:T(8,128)(2,1)S(1)} collective-permute-done((bf16[2,256,128]{2,1,0:T(8,128)(2,1)S(1)}, bf16[2,256,128]{2,1,0:T(8,128)(2,1)S(1)}, u32[]{:S(2)}, u32[]{:S(2)}) %collective-permute-start.12) | collective-permute-done | bytes 131104 | tf_op jit(solution)/shard_map/ppermute | solution.py:353
  55.5 0.0 collective-permute-done.13.refs_3_
  55.5 0.1 key_sum.1
  55.5 0.0 collective-permute-done.17.dq_pair
  55.6 0.1 collective-permute-start.18
  55.6 1.4 %collective-permute-done.18.sib_ref = bf16[2,384,128]{2,1,0:T(8,128)(2,1)S(1)} collective-permute-done((bf16[2,384,128]{2,1,0:T(8,128)(2,1)S(1)}, bf16[2,384,128]{2,1,0:T(8,128)(2,1)S(1)}, u32[]{:S(2)}, u32[]{:S(2)}) %collective-permute-start.18) | collective-permute-done | bytes 196640 | tf_op jit(solution)/shard_map/ppermute | solution.py:353
  57.1 0.8 %finish.1 = (bf16[1,128,512]{2,1,0:T(8,128)(2,1)}, bf16[1,128,512]{2,1,0:T(8,128)(2,1)}, bf16[1,128,512]{2,1,0:T(8,128)(2,1)}) custom-call(bf16[2,256,128]{2,1,0:T(8,128)(2,1)S(1)} %get-tuple-element.54.dkv_own, bf16[2,128,128]{2,1,0:T(8,128)(2,1)S(1)} %get-tuple-element.60.dq_same, bf16[2,128,128]{2,1,0:T(8,128)(2,1)S(1)} %collective-permute-done.17.dq_pair, ...), custom_call_target="tpu_custom_call" | custom-call | tf_op jit(solution)/shard_map/finish/pallas_call | solution.py:513
  (4 shorter events, 0.1 us)
Async XLA Ops:
  0.6 0.7 %copy-start.2 = (s32[1,1,24]{2,1,0:T(1,128)S(1)}, s32[1,1,24]{2,1,0:T(1,128)}, u32[]{:S(2)}) copy-start(s32[1,1,24]{2,1,0:T(1,128)} %slot_ref.1) | copy-start | bytes 292
  1.3 0.8 %copy-start.1 = (f32[1,8,1024]{2,1,0:T(8,128)S(1)}, f32[1,8,1024]{2,1,0:T(8,128)}, u32[]{:S(2)}) copy-start(f32[1,8,1024]{2,1,0:T(8,128)} %lse_hbm.1) | copy-start | bytes 98308
  4.4 5.0 %collective-permute-start = (bf16[784,128]{1,0:T(8,128)(2,1)}, bf16[784,128]{1,0:T(8,128)(2,1)S(1)}, u32[]{:S(2)}, u32[]{:S(2)}) collective-permute-start(bf16[784,128]{1,0:T(8,128)(2,1)} %get-tuple-element.34), channel_id=1, source_target_pairs={{0,1},{1,0},{2,3},{3,2},{4,5},{5,4},{6,7},{7,6},{8,9},{9,8},{10,11... | collective-permute-start | bytes 602120 | tf_op jit(solution)/shard_map/ppermute | solution.py:353
  5.0 8.5 %collective-permute-start.1 = (bf16[272,128]{1,0:T(8,128)(2,1)S(1)}, bf16[272,128]{1,0:T(8,128)(2,1)S(1)}, u32[]{:S(2)}, u32[]{:S(2)}) collective-permute-start(bf16[272,128]{1,0:T(8,128)(2,1)S(1)} %get-tuple-element.35), channel_id=1, source_target_pairs={{0,8},{1,9},{8,0},{9,1},{16,24},{17,25},{24,16},{25,17},{2,10},{3,... | collective-permute-start | bytes 208904 | tf_op jit(solution)/shard_map/ppermute | solution.py:353
  7.6 5.8 %collective-permute-start.2 = (bf16[272,128]{1,0:T(8,128)(2,1)S(1)}, bf16[272,128]{1,0:T(8,128)(2,1)S(1)}, u32[]{:S(2)}, u32[]{:S(2)}) collective-permute-start(bf16[272,128]{1,0:T(8,128)(2,1)S(1)} %get-tuple-element.36), channel_id=1, source_target_pairs={{0,9},{1,8},{8,1},{9,0},{16,25},{17,24},{24,17},{25,16},{2,11},{3,... | collective-permute-start | bytes 208904 | tf_op jit(solution)/shard_map/ppermute | solution.py:353
  7.7 5.7 %collective-permute-start.3 = (s32[15,8,128]{2,1,0:T(8,128)S(1)}, s32[15,8,128]{2,1,0:T(8,128)S(1)}, u32[]{:S(2)}, u32[]{:S(2)}) collective-permute-start(s32[15,8,128]{2,1,0:T(8,128)S(1)} %get-tuple-element.37.bits_own), channel_id=1, source_target_pairs={{0,8},{8,0},{16,24},{24,16},{1,9},{9,1},{17,25},{25,17},{2,10},{10... | collective-permute-start | bytes 184328 | tf_op jit(solution)/shard_map/ppermute | solution.py:353
  9.4 0.9 %copy-start = (bf16[512,128]{1,0:T(8,128)(2,1)S(1)}, bf16[512,128]{1,0:T(8,128)(2,1)}, u32[]{:S(2)}) copy-start(bf16[512,128]{1,0:T(8,128)(2,1)} %get-tuple-element.40.kv_own) | copy-start | bytes 393220
  10.4 12.9 %collective-permute-start.7 = (bf16[2,256,128]{2,1,0:T(8,128)(2,1)S(1)}, bf16[2,256,128]{2,1,0:T(8,128)(2,1)S(1)}, u32[]{:S(2)}, u32[]{:S(2)}) collective-permute-start(bf16[2,256,128]{2,1,0:T(8,128)(2,1)S(1)} %get-tuple-element.41.same_ref), channel_id=1, source_target_pairs={{0,16},{8,24},{16,0},{24,8},{1,17},{9,25},{17,1},{25,9},{2,18},{10... | collective-permute-start | bytes 393224 | tf_op jit(solution)/shard_map/ppermute | solution.py:353
  13.0 10.3 %collective-permute-start.8 = (bf16[2,256,128]{2,1,0:T(8,128)(2,1)S(1)}, bf16[2,256,128]{2,1,0:T(8,128)(2,1)S(1)}, u32[]{:S(2)}, u32[]{:S(2)}) collective-permute-start(bf16[2,256,128]{2,1,0:T(8,128)(2,1)S(1)} %get-tuple-element.42.pair_ref), channel_id=1, source_target_pairs={{0,24},{8,16},{16,8},{24,0},{1,25},{9,17},{17,9},{25,1},{2,26},{10... | collective-permute-start | bytes 393224 | tf_op jit(solution)/shard_map/ppermute | solution.py:353
  13.5 15.5 %collective-permute-start.6 = (bf16[4,272,128]{2,1,0:T(8,128)(2,1)S(1)}, bf16[4,272,128]{2,1,0:T(8,128)(2,1)S(1)}, u32[]{:S(2)}, u32[]{:S(2)}) collective-permute-start(bf16[4,272,128]{2,1,0:T(8,128)(2,1)S(1)} %get-tuple-element.39.refs_0_), channel_id=1, source_target_pairs={{0,6},{2,4},{4,2},{6,0},{1,7},{3,5},{5,3},{7,1},{8,14},{10,12},{12... | collective-permute-start | bytes 835592 | tf_op jit(solution)/shard_map/ppermute | solution.py:353
  16.0 13.0 %collective-permute-start.5 = (bf16[4,272,128]{2,1,0:T(8,128)(2,1)S(1)}, bf16[4,272,128]{2,1,0:T(8,128)(2,1)S(1)}, u32[]{:S(2)}, u32[]{:S(2)}) collective-permute-start(bf16[4,272,128]{2,1,0:T(8,128)(2,1)S(1)} %get-tuple-element.39.refs_0_), channel_id=1, source_target_pairs={{0,4},{2,6},{4,0},{6,2},{1,5},{3,7},{5,1},{7,3},{8,12},{10,14},{12... | collective-permute-start | bytes 835592 | tf_op jit(solution)/shard_map/ppermute | solution.py:353
  16.5 12.5 %collective-permute-start.4 = (bf16[4,272,128]{2,1,0:T(8,128)(2,1)S(1)}, bf16[4,272,128]{2,1,0:T(8,128)(2,1)S(1)}, u32[]{:S(2)}, u32[]{:S(2)}) collective-permute-start(bf16[4,272,128]{2,1,0:T(8,128)(2,1)S(1)} %get-tuple-element.39.refs_0_), channel_id=1, source_target_pairs={{0,2},{2,0},{4,6},{6,4},{1,3},{3,1},{5,7},{7,5},{8,10},{10,8},{12,... | collective-permute-start | bytes 835592 | tf_op jit(solution)/shard_map/ppermute | solution.py:353
  23.3 5.5 %collective-permute-start.9 = (bf16[2,256,128]{2,1,0:T(8,128)(2,1)S(1)}, bf16[2,256,128]{2,1,0:T(8,128)(2,1)S(1)}, u32[]{:S(2)}, u32[]{:S(2)}) collective-permute-start(bf16[2,256,128]{2,1,0:T(8,128)(2,1)S(1)} %get-tuple-element.43), channel_id=1, source_target_pairs={{0,8},{8,0},{16,24},{24,16},{1,9},{9,1},{17,25},{25,17},{2,10},{10... | collective-permute-start | bytes 393224 | tf_op jit(solution)/shard_map/ppermute | solution.py:353
  25.9 3.1 %collective-permute-start.10 = (s32[2,13,8,128]{3,2,1,0:T(8,128)S(1)}, s32[2,13,8,128]{3,2,1,0:T(8,128)S(1)}, u32[]{:S(2)}, u32[]{:S(2)}) collective-permute-start(s32[2,13,8,128]{3,2,1,0:T(8,128)S(1)} %get-tuple-element.48.refs_7_), channel_id=1, source_target_pairs={{0,1},{1,0},{2,3},{3,2},{4,5},{5,4},{6,7},{7,6},{8,9},{9,8},{10,11... | collective-permute-start | bytes 319496 | tf_op jit(solution)/shard_map/ppermute | solution.py:353
  34.9 10.7 %collective-permute-start.14 = (bf16[4,128,128]{2,1,0:T(8,128)(2,1)S(1)}, bf16[4,128,128]{2,1,0:T(8,128)(2,1)S(1)}, u32[]{:S(2)}, u32[]{:S(2)}) collective-permute-start(bf16[4,128,128]{2,1,0:T(8,128)(2,1)S(1)} %get-tuple-element.57), channel_id=1, source_target_pairs={{0,6},{2,4},{4,2},{6,0},{1,7},{3,5},{5,3},{7,1},{8,14},{10,12},{12... | collective-permute-start | bytes 393224 | tf_op jit(solution)/shard_map/ppermute | solution.py:353
  36.3 9.8 %collective-permute-start.15 = (bf16[4,128,128]{2,1,0:T(8,128)(2,1)S(1)}, bf16[4,128,128]{2,1,0:T(8,128)(2,1)S(1)}, u32[]{:S(2)}, u32[]{:S(2)}) collective-permute-start(bf16[4,128,128]{2,1,0:T(8,128)(2,1)S(1)} %get-tuple-element.58), channel_id=1, source_target_pairs={{0,4},{2,6},{4,0},{6,2},{1,5},{3,7},{5,1},{7,3},{8,12},{10,14},{12... | collective-permute-start | bytes 393224 | tf_op jit(solution)/shard_map/ppermute | solution.py:353
  41.2 5.0 %collective-permute-start.16 = (bf16[4,128,128]{2,1,0:T(8,128)(2,1)S(1)}, bf16[4,128,128]{2,1,0:T(8,128)(2,1)S(1)}, u32[]{:S(2)}, u32[]{:S(2)}) collective-permute-start(bf16[4,128,128]{2,1,0:T(8,128)(2,1)S(1)} %get-tuple-element.59), channel_id=1, source_target_pairs={{0,2},{2,0},{4,6},{6,4},{1,3},{3,1},{5,7},{7,5},{8,10},{10,8},{12,... | collective-permute-start | bytes 393224 | tf_op jit(solution)/shard_map/ppermute | solution.py:353
  41.2 8.2 %collective-permute-start.11 = (bf16[2,256,128]{2,1,0:T(8,128)(2,1)S(1)}, bf16[2,256,128]{2,1,0:T(8,128)(2,1)S(1)}, u32[]{:S(2)}, u32[]{:S(2)}) collective-permute-start(bf16[2,256,128]{2,1,0:T(8,128)(2,1)S(1)} %get-tuple-element.51), channel_id=1, source_target_pairs={{0,24},{8,16},{16,8},{24,0},{1,25},{9,17},{17,9},{25,1},{2,26},{10... | collective-permute-start | bytes 393224 | tf_op jit(solution)/shard_map/ppermute | solution.py:353
  45.0 10.4 %collective-permute-start.12 = (bf16[2,256,128]{2,1,0:T(8,128)(2,1)S(1)}, bf16[2,256,128]{2,1,0:T(8,128)(2,1)S(1)}, u32[]{:S(2)}, u32[]{:S(2)}) collective-permute-start(bf16[2,256,128]{2,1,0:T(8,128)(2,1)S(1)} %get-tuple-element.52), channel_id=1, source_target_pairs={{0,16},{8,24},{16,0},{24,8},{1,17},{9,25},{17,1},{25,9},{2,18},{10... | collective-permute-start | bytes 393224 | tf_op jit(solution)/shard_map/ppermute | solution.py:353
  45.5 9.9 %collective-permute-start.13 = (bf16[2,256,128]{2,1,0:T(8,128)(2,1)S(1)}, bf16[2,256,128]{2,1,0:T(8,128)(2,1)S(1)}, u32[]{:S(2)}, u32[]{:S(2)}) collective-permute-start(bf16[2,256,128]{2,1,0:T(8,128)(2,1)S(1)} %get-tuple-element.53), channel_id=1, source_target_pairs={{0,8},{8,0},{16,24},{24,16},{1,9},{9,1},{17,25},{25,17},{2,10},{10... | collective-permute-start | bytes 393224 | tf_op jit(solution)/shard_map/ppermute | solution.py:353
  46.2 9.3 %collective-permute-start.17 = (bf16[2,128,128]{2,1,0:T(8,128)(2,1)S(1)}, bf16[2,128,128]{2,1,0:T(8,128)(2,1)S(1)}, u32[]{:S(2)}, u32[]{:S(2)}) collective-permute-start(bf16[2,128,128]{2,1,0:T(8,128)(2,1)S(1)} %get-tuple-element.61), channel_id=1, source_target_pairs={{0,8},{8,0},{16,24},{24,16},{1,9},{9,1},{17,25},{25,17},{2,10},{10... | collective-permute-start | bytes 196616 | tf_op jit(solution)/shard_map/ppermute | solution.py:353
  55.6 1.5 %collective-permute-start.18 = (bf16[2,384,128]{2,1,0:T(8,128)(2,1)S(1)}, bf16[2,384,128]{2,1,0:T(8,128)(2,1)S(1)}, u32[]{:S(2)}, u32[]{:S(2)}) collective-permute-start(bf16[2,384,128]{2,1,0:T(8,128)(2,1)S(1)} %bundle.1), channel_id=1, source_target_pairs={{0,1},{1,0},{2,3},{3,2},{4,5},{5,4},{6,7},{7,6},{8,9},{9,8},{10,11... | collective-permute-start | bytes 589832 | tf_op jit(solution)/shard_map/ppermute | solution.py:353
